TPU v7x, 256 devices: a whole 4x4x8 slice. The times are simulated.
256 devices in a mesh: section: 4 (over x), dp: 4 (over z_hi), tensor: 16 (over y, z_lo, core).
Axes of the slice: x: 4, y: 4, z: 8 (z_hi: 4, z_lo: 2; z = z_hi * 2 + z_lo), core: 2. Of those that a mesh axis runs over, the one named last changes fastest.
Arguments:
- act_input: bfloat16 [4, 2048, 14336], P('section', 'tensor', 'dp'), may hold values from -400 to 400
- ln_gain: float32 [4, 14336], P('section', 'dp'), may hold values from 0.1 to 1.9
- ln_shift: float32 [4, 14336], P('section', 'dp'), may hold values from -3 to 3
- w_proj: bfloat16 [4, 14336, 14336], P('section', 'dp', 'tensor'), may hold values from -0.046875 to 0.046875
- b_proj: float32 [4, 14336], P('section', 'tensor'), may hold values from -3 to 3
- act_ids: int32 [2048], P('dp'), may hold values from 0 to 127
- sent_copy: bfloat16 [4, 512, 14336], P('section', 'dp', 'tensor'), may hold values from -64 to 64
- held_copy: bfloat16 [4, 512, 14336], P('section', 'dp', 'tensor'), may hold values from -6 to 6
- grad_input: bfloat16 [4, 2048, 14336], P('section', 'tensor', 'dp'), may hold values from -6 to 6
- grad_ids: int32 [2048], P('tensor'), may hold values from 0 to 127
- back_sent: bfloat16 [4, 2048, 14336], P('section', 'tensor', 'dp'), may hold values from -64 to 64
- back_held: bfloat16 [4, 2048, 14336], P('section', 'tensor', 'dp'), may hold values from -6 to 6
Outputs:
- arrived: bfloat16 [4, 2048, 14336], P('section', 'dp', 'tensor')
- grad_arrived: bfloat16 [4, 2048, 14336], P('section', 'tensor', 'dp')
Inputs may be any that keep to these rules, and one draw needn't show every extreme that they name: `act_ids`: a slot within the block of 128 activation store rows of the token's data group. `grad_ids`: a slot within the block of 128 gradient store rows of the token's block of 128 tokens.
All inputs are finite; a program needn't handle non-finite values.
Results may differ from a plain program's by a relative error of at most 0.015.
Values may be sent and summed in bfloat16 or wider, within the bound.
A program may use at most 128 MiB of HBM per device.

v0:
```python
import math

import jax
import jax.numpy as jnp
from jax import lax
from jax.sharding import PartitionSpec as P

D = 14336
HB = 128


epsilon = 1e-05
scale_epsilon = 1e-06
clip_level = 2.5


def from_behind(value, axis, steps):
    count = lax.axis_size(axis)
    pairs = [(source, (source + steps) % count) for source in range(count)]
    return lax.ppermute(value, axis, pairs)


def hadamard_table(order):
    index = jnp.arange(order, dtype=jnp.int32)
    common = jnp.bitwise_and(index[:, None], index[None, :])
    parity = jnp.zeros_like(common)
    for bit in range(order.bit_length()):
        parity = parity + jnp.bitwise_and(jnp.right_shift(common, bit), 1)
    signs = 1.0 - 2.0 * jnp.remainder(parity, 2).astype(jnp.float32)
    return signs / math.sqrt(order)


def rotate(values):
    table = hadamard_table(HB)
    leading = values.shape[0]
    blocks = values.reshape(leading, -1, HB)
    turned = jnp.einsum("rbk,kl->rbl", blocks, table, precision=lax.Precision.HIGHEST)
    return turned.reshape(values.shape)


def encode(delta):
    leading = delta.shape[0]
    turned = rotate(delta).reshape(leading, -1, HB)
    block_scale = jnp.sqrt(jnp.mean(turned * turned, axis=2) + scale_epsilon).astype(jnp.bfloat16)
    levels = jnp.clip(turned / block_scale.astype(jnp.float32)[:, :, None], -clip_level, clip_level)
    return (levels.astype(jnp.bfloat16).reshape(delta.shape), block_scale)


def decode(held_rows, coded, block_scale):
    leading = coded.shape[0]
    spread = (
        coded.astype(jnp.float32).reshape(leading, -1, HB)
        * block_scale.astype(jnp.float32)[:, :, None]
    )
    return (held_rows.astype(jnp.float32) + rotate(spread.reshape(coded.shape))).astype(
        jnp.bfloat16
    )


def shards(
    act_input,
    ln_gain,
    ln_shift,
    w_proj,
    b_proj,
    act_ids,
    sent_copy,
    held_copy,
    grad_input,
    grad_ids,
    back_sent,
    back_held,
):
    values = act_input[0].astype(jnp.float32)
    totals = lax.psum((jnp.sum(values, axis=1), jnp.sum(values * values, axis=1)), "dp")
    row_mean = totals[0] / D
    row_var = totals[1] / D - row_mean * row_mean
    normed = (
        (values - row_mean[:, None]) * lax.rsqrt(row_var + epsilon)[:, None] * ln_gain[0]
        + ln_shift[0]
    ).astype(jnp.bfloat16)
    weights = w_proj[0]
    partial_value = jnp.dot(
        lax.all_gather(normed, "tensor", axis=0, tiled=True),
        weights,
        preferred_element_type=jnp.float32,
    )
    output = lax.psum_scatter(
        partial_value.astype(jnp.bfloat16), "dp", scatter_dimension=0, tiled=True
    ).astype(jnp.float32)
    output = output + b_proj[0]
    delta = output - jnp.take(sent_copy[0], act_ids, axis=0).astype(jnp.float32)
    wire, block_scale = encode(delta)
    grad_delta = grad_input[0].astype(jnp.float32) - jnp.take(
        back_sent[0], grad_ids, axis=0
    ).astype(jnp.float32)
    grad_wire, grad_scale = encode(grad_delta)
    came, came_scale = from_behind((wire, block_scale), "section", 1)
    grad_came, grad_came_scale = from_behind((grad_wire, grad_scale), "section", -1)
    arrived = decode(jnp.take(held_copy[0], act_ids, axis=0), came, came_scale)
    grad_arrived = decode(jnp.take(back_held[0], grad_ids, axis=0), grad_came, grad_came_scale)
    return (arrived[None], grad_arrived[None])


def solution(mesh):
    placed = (
        P("section", "tensor", "dp"),
        P("section", "dp"),
        P("section", "dp"),
        P("section", "dp", "tensor"),
        P("section", "tensor"),
        P("dp"),
        P("section", "dp", "tensor"),
        P("section", "dp", "tensor"),
        P("section", "tensor", "dp"),
        P("tensor"),
        P("section", "tensor", "dp"),
        P("section", "tensor", "dp"),
    )
    return jax.shard_map(
        shards,
        mesh=mesh,
        in_specs=placed,
        out_specs=(P("section", "dp", "tensor"), P("section", "tensor", "dp")),
        check_vma=False,
    )
```

profile of v0, /device:TPU:32, one launch (start us, length us, event | category | flops | bytes accessed | tf_op | source)
XLA Modules:
  0.0 251.0 jit_solution(360320756092187554)
XLA Ops:
  7.2 0.0 copy-start
  7.2 0.0 copy-start.4
  7.2 0.0 all-gather.2.cloned.1.call-start
  7.3 1.5 convert_reduce_fusion
  8.8 1.4 fusion.11
  10.2 0.0 copy-done.8
  10.3 0.0 copy-done.9
  10.3 14.0 %all-reduce = (f32[128]{0:T(128)S(1)}, f32[128]{0:T(128)S(1)}) all-reduce(f32[128]{0:T(128)S(1)} %fusion.11, f32[128]{0:T(128)S(1)} %convert_reduce_fusion), channel_id=1, replica_groups=mesh['section'=4,'dp'=4,'tensor'=16] {'dp'}, use_global_device_ids=true, to_apply=%region_3.5 | all-reduce | flops 256 | bytes 2048 | tf_op jit(solution)/shard_map/psum | solution.py:75
  24.4 1.4 fusion.10
  25.7 0.0 all-gather.2.cloned.1.call-update
  25.7 0.0 reduce-scatter.2.cloned.1.call-start
  25.8 83.1 %all-gather.2.cloned.1.call-done = bf16[2048,3584]{1,0:T(8,128)(2,1)} async-done(((bf16[128,3584]{1,0:T(8,128)(2,1)}), bf16[2048,3584]{1,0:T(8,128)(2,1)}) %all-gather.2.cloned.1.call-update) | async-done | bytes 14680080 | tf_op jit(solution)/shard_map/all_gather | solution.py:84
  108.9 20.7 %fusion.2 = bf16[2048,896]{1,0:T(8,128)(2,1)} fusion(bf16[2048,3584]{1,0:T(8,128)(2,1)} %all-gather.2.cloned.1.call-done, bf16[1,3584,896]{2,1,0:T(8,128)(2,1)} %param.19), kind=kOutput, calls=%fused_computation.6 | convolution fusion | flops 13155172352 | bytes 24772608 | tf_op jit(solution)/shard_map/dot_general | solution.py:83
  129.6 0.0 reduce-scatter.2.cloned.1.call-update
  129.6 0.6 copy-done.12
  130.2 0.0 copy-start.7
  130.3 1.1 gather_fusion.3
  131.4 0.0 copy-done.7
  131.4 1.6 convert_subtract_fusion
  133.0 1.8 copy.22
  134.8 1.9 multiply_reduce_fusion
  136.7 0.0 copy-start.10
  136.7 0.0 copy-start.11
  136.8 0.0 copy-start.1
  136.8 0.2 clamp_convert_fusion
  137.0 2.8 %collective-permute-start.2 = (bf16[128,3584]{0,1:T(8,128)(2,1)S(1)}, bf16[128,3584]{0,1:T(8,128)(2,1)}, u32[]{:S(2)}, u32[]{:S(2)}) collective-permute-start(bf16[128,3584]{0,1:T(8,128)(2,1)S(1)} %bitcast.63), channel_id=1, source_target_pairs={{0,192},{64,0},{128,64},{192,128},{1,193},{65,1},{129,65},{193,129... | collective-permute-start | bytes 2752520 | tf_op jit(solution)/shard_map/ppermute | solution.py:20
  139.8 0.8 collective-permute-start.3
  140.7 0.0 copy-start.2
  140.8 2.7 %gather_fusion.1 = bf16[512,896]{1,0:T(8,128)(2,1)} fusion(bf16[128,896]{1,0:T(8,128)(2,1)S(1)} %bitcast.56, s32[1024]{0:T(1024)S(1)} %pad_clamp_fusion.1), kind=kCustom, calls=%fused_computation.2.clone | custom fusion | bytes 1837056 | tf_op jit(solution)/shard_map/jit(_take)/gather | solution.py:92
  143.5 2.7 %gather_fusion = bf16[512,896]{1,0:T(8,128)(2,1)} fusion(bf16[128,896]{1,0:T(8,128)(2,1)S(1)} %bitcast.57, s32[1024]{0:T(1024)S(1)} %pad_clamp_fusion.1), kind=kCustom, calls=%fused_computation.clone | custom fusion | bytes 1837056 | tf_op jit(solution)/shard_map/jit(_take)/gather | solution.py:100
  146.2 2.0 gather_fusion.2
  148.3 11.8 %collective-permute-done.3 = bf16[128,28]{0,1:T(8,128)(2,1)S(1)} collective-permute-done((bf16[128,28]{0,1:T(8,128)(2,1)S(1)}, bf16[128,28]{0,1:T(8,128)(2,1)S(1)}, u32[]{:S(2)}, u32[]{:S(2)}) %collective-permute-start.3) | collective-permute-done | bytes 7200 | tf_op jit(solution)/shard_map/ppermute | solution.py:20
  160.0 0.0 collective-permute-done.2
  160.0 3.1 %fusion.12 = f32[128,28,128]{0,2,1:T(8,128)S(1)} fusion(bf16[128,28,128]{0,2,1:T(8,128)(2,1)} %bitcast.20, f32[128,28]{0,1:T(8,128)S(1)} %convert_element_type.113), kind=kOutput, calls=%fused_computation.17 | convolution fusion | flops 706199552 | bytes 2766848 | tf_op jit(solution)/shard_map/rbk,kl->rbl/dot_general | solution.py:37
  163.2 1.7 copy.25
  164.9 40.8 %reduce-scatter.2.cloned.1.call-done = bf16[512,896]{1,0:T(8,128)(2,1)} async-done(((bf16[2048,896]{1,0:T(8,128)(2,1)}), bf16[512,896]{1,0:T(8,128)(2,1)}) %reduce-scatter.2.cloned.1.call-update) | async-done | bytes 917520 | tf_op jit(solution)/shard_map/reduce_scatter | solution.py:88
  205.7 1.8 convert_subtract_fusion.1
  207.5 1.8 copy.18
  209.2 3.5 %multiply_reduce_fusion.1 = (f32[512,7]{0,1:T(8,128)S(1)}, f32[512,7,128]{0,2,1:T(8,128)S(1)}) fusion(f32[512,7,128]{0,2,1:T(8,128)} %bitcast.60), kind=kOutput, calls=%fused_computation.26 | convolution fusion | flops 706195968 | bytes 3684352 | tf_op jit(solution)/shard_map/rbk,kl->rbl/dot_general | solution.py:37
  212.8 0.3 clamp_convert_fusion.1
  213.1 1.5 collective-permute-start
  214.5 1.5 collective-permute-start.1
  216.1 1.2 fusion.15
  217.3 19.4 %collective-permute-done.1 = bf16[512,7]{0,1:T(8,128)(2,1)S(1)} collective-permute-done((bf16[512,7]{0,1:T(8,128)(2,1)S(1)}, bf16[512,7]{0,1:T(8,128)(2,1)S(1)}, u32[]{:S(2)}, u32[]{:S(2)}) %collective-permute-start.1) | collective-permute-done | bytes 7200 | tf_op jit(solution)/shard_map/ppermute | solution.py:20
  236.7 0.0 collective-permute-done
  236.7 3.3 %fusion.13 = f32[512,7,128]{0,2,1:T(8,128)} fusion(bf16[512,7,128]{0,2,1:T(8,128)(2,1)S(1)} %bitcast.65, f32[512,7]{0,1:T(8,128)S(1)} %convert_element_type.104), kind=kOutput, calls=%fused_computation.20 | convolution fusion | flops 706199552 | bytes 2766848 | tf_op jit(solution)/shard_map/rbk,kl->rbl/dot_general | solution.py:37
  240.0 1.8 copy.21
  241.8 2.4 fusion.14
  (29 shorter events, 0.2 us)
Async XLA Ops:
  7.2 123.1 %copy-start = (bf16[1,128,3584]{2,1,0:T(8,128)(2,1)S(1)}, bf16[1,128,3584]{2,1,0:T(8,128)(2,1)}, u32[]{:S(2)}) copy-start(bf16[1,128,3584]{2,1,0:T(8,128)(2,1)} %param.26) | copy-start | bytes 2752516
  7.2 17.2 %copy-start.4 = (bf16[1,128,3584]{2,1,0:T(8,128)(2,1)S(1)}, bf16[1,128,3584]{2,1,0:T(8,128)(2,1)}, u32[]{:S(2)}) copy-start(bf16[1,128,3584]{2,1,0:T(8,128)(2,1)} %param.16) | copy-start | bytes 2752516
  7.2 3.0 %copy-start.8 = (f32[1,3584]{1,0:T(1,128)S(1)}, f32[1,3584]{1,0:T(1,128)}, u32[]{:S(2)}) copy-start(f32[1,3584]{1,0:T(1,128)} %param.17) | copy-start | bytes 43012
  7.2 3.1 %copy-start.9 = (f32[1,3584]{1,0:T(1,128)S(1)}, f32[1,3584]{1,0:T(1,128)}, u32[]{:S(2)}) copy-start(f32[1,3584]{1,0:T(1,128)} %param.18) | copy-start | bytes 43012
  7.2 101.7 %all-gather.2.cloned.1.call-start = ((), (), s32[]{:S(2)}) async-start(), calls=%async_computation.1 | async-start | bytes 15597568 | tf_op jit(solution)/shard_map/all_gather | solution.py:84
  25.7 179.9 %reduce-scatter.2.cloned.1.call-start = ((), (), s32[]{:S(2)}) async-start(), calls=%async_computation.2 | async-start | bytes 4587520 | tf_op jit(solution)/shard_map/reduce_scatter | solution.py:88
  129.6 0.7 copy-start.12
  130.2 1.2 copy-start.7
  136.7 3.9 %copy-start.10 = (s32[512]{0:T(512)S(1)}, s32[512]{0:T(512)}, u32[]{:S(2)}) copy-start(s32[512]{0:T(512)} %param.21) | copy-start | bytes 6148
  136.7 4.0 %copy-start.11 = (f32[1,896]{1,0:T(1,128)S(1)}, f32[1,896]{1,0:T(1,128)}, u32[]{:S(2)}) copy-start(f32[1,896]{1,0:T(1,128)} %param.20) | copy-start | bytes 10756
  136.8 4.0 %copy-start.1 = (bf16[1,128,896]{2,1,0:T(8,128)(2,1)S(1)}, bf16[1,128,896]{2,1,0:T(8,128)(2,1)}, u32[]{:S(2)}) copy-start(bf16[1,128,896]{2,1,0:T(8,128)(2,1)} %param.22) | copy-start | bytes 688132
  137.0 23.0 %collective-permute-start.2 = (bf16[128,3584]{0,1:T(8,128)(2,1)S(1)}, bf16[128,3584]{0,1:T(8,128)(2,1)}, u32[]{:S(2)}, u32[]{:S(2)}) collective-permute-start(bf16[128,3584]{0,1:T(8,128)(2,1)S(1)} %bitcast.63), channel_id=1, source_target_pairs={{0,192},{64,0},{128,64},{192,128},{1,193},{65,1},{129,65},{193,129... | collective-permute-start | bytes 2752520 | tf_op jit(solution)/shard_map/ppermute | solution.py:20
  139.8 20.2 %collective-permute-start.3 = (bf16[128,28]{0,1:T(8,128)(2,1)S(1)}, bf16[128,28]{0,1:T(8,128)(2,1)S(1)}, u32[]{:S(2)}, u32[]{:S(2)}) collective-permute-start(bf16[128,28]{0,1:T(8,128)(2,1)S(1)} %get-tuple-element.7), channel_id=1, source_target_pairs={{0,192},{64,0},{128,64},{192,128},{1,193},{65,1},{129,65},{193,129... | collective-permute-start | bytes 21512 | tf_op jit(solution)/shard_map/ppermute | solution.py:20
  140.7 2.8 %copy-start.2 = (bf16[1,128,896]{2,1,0:T(8,128)(2,1)S(1)}, bf16[1,128,896]{2,1,0:T(8,128)(2,1)}, u32[]{:S(2)}) copy-start(bf16[1,128,896]{2,1,0:T(8,128)(2,1)} %param.23) | copy-start | bytes 688132
  143.5 2.7 %copy-start.3 = (bf16[1,128,3584]{2,1,0:T(8,128)(2,1)S(1)}, bf16[1,128,3584]{2,1,0:T(8,128)(2,1)}, u32[]{:S(2)}) copy-start(bf16[1,128,3584]{2,1,0:T(8,128)(2,1)} %param.27) | copy-start | bytes 2752516
  212.7 3.3 %copy-start.5 = (f32[128,3584]{1,0:T(8,128)S(1)}, f32[128,3584]{1,0:T(8,128)}, u32[]{:S(2)}) copy-start(f32[128,3584]{1,0:T(8,128)} %copy.25) | copy-start | bytes 5505028
  212.7 3.3 %copy-start.6 = (bf16[128,3584]{1,0:T(8,128)(2,1)S(1)}, bf16[128,3584]{1,0:T(8,128)(2,1)}, u32[]{:S(2)}) copy-start(bf16[128,3584]{1,0:T(8,128)(2,1)} %gather_fusion.2) | copy-start | bytes 2752516
  213.1 23.6 %collective-permute-start = (bf16[512,896]{0,1:T(8,128)(2,1)S(1)}, bf16[512,896]{0,1:T(8,128)(2,1)S(1)}, u32[]{:S(2)}, u32[]{:S(2)}) collective-permute-start(bf16[512,896]{0,1:T(8,128)(2,1)S(1)} %bitcast.64), channel_id=1, source_target_pairs={{0,64},{64,128},{128,192},{192,0},{1,65},{65,129},{129,193},{193,1... | collective-permute-start | bytes 2752520 | tf_op jit(solution)/shard_map/ppermute | solution.py:20
  214.5 22.1 %collective-permute-start.1 = (bf16[512,7]{0,1:T(8,128)(2,1)S(1)}, bf16[512,7]{0,1:T(8,128)(2,1)S(1)}, u32[]{:S(2)}, u32[]{:S(2)}) collective-permute-start(bf16[512,7]{0,1:T(8,128)(2,1)S(1)} %get-tuple-element.9), channel_id=1, source_target_pairs={{0,64},{64,128},{128,192},{192,0},{1,65},{65,129},{129,193},{193,1... | collective-permute-start | bytes 21512 | tf_op jit(solution)/shard_map/ppermute | solution.py:20
Sparse Core Ops, SparseCore 0:
  25.9 82.9 all-gather.1
  129.7 75.9 reduce-scatter.1
where the time goes:
time: 253 us; the launch traced here: 251 us
  waiting for transfers between devices  155 us (61%)
  matrix products  32.6 us (13%)
  local copies, waits for them, and re-layouts  16.4 us (6%)
  between operations  14.3 us (6%)
  blocking collectives  14 us (6%)
  other arithmetic  12 us (5%)
  starting transfers between devices  6.71 us (3%)
    all_gather x1, waiting for transfers between devices, shards(): lax.all_gather(normed, 'tensor', axis=0, tiled=True)  83.1 us
    reduce_scatter x1, waiting for transfers between devices, shards(): lax.psum_scatter(partial_value.astype(jnp.bfloat16), 'dp', scatter_dimens...  40.8 us
    ppermute x4, waiting for transfers between devices, from_behind(): return lax.ppermute(value, axis, pairs)  31.1 us
    dot_general x1, matrix products, shards(): jnp.dot(lax.all_gather(normed, 'tensor', axis=0, tiled=True), weights, pr...  20.7 us
    psum x1, blocking collectives, shards(): lax.psum((jnp.sum(values, axis=1), jnp.sum(values * values, axis=1)), 'dp')  14 us
    dot_general x4, matrix products, rotate(): jnp.einsum('rbk,kl->rbl', blocks, table, precision=lax.Precision.HIGHEST)  11.9 us
    ppermute x4, starting transfers between devices, from_behind(): return lax.ppermute(value, axis, pairs)  6.63 us
  transfers between devices with their start and end apart: 6, of which 4 were waited for; matrix products, arithmetic and copies ran while one was open for 8% of the time, Pallas kernels for 0%

commit v1 on v0

v1 whole, which is shorter than its diff:
```python
import functools
import math

import jax
import jax.numpy as jnp
from jax import lax
from jax.experimental import pallas as pl
from jax.experimental.pallas import tpu as pltpu
from jax.sharding import PartitionSpec as P

D = 14336
HB = 128
KD = 3584
ND = 896
TR = 128
PIECES = 8
PR = TR // PIECES
PLANE = 8 * PR
GB = 4
GSTEPS = KD // (HB * GB)
GC = GB * HB

epsilon = 1e-05
scale_epsilon = 1e-06
clip_level = 2.5

MESH = pl.DeviceIdType.MESH
f32 = jnp.float32
bf16 = jnp.bfloat16


def dot(a, b):
    return jnp.dot(a, b, preferred_element_type=f32)


def clipped(tu):
    mean = jnp.sum(tu * tu, axis=1, keepdims=True) * (1.0 / (HB * HB))
    scale = jnp.sqrt(mean + scale_epsilon).astype(bf16).astype(f32)
    bound = scale * (clip_level / math.sqrt(HB))
    return jnp.clip(tu * (1.0 / HB), -bound, bound).astype(bf16)


def kernel(
    x_hbm, gain, shift, w_hbm, bias, aids, sent_hbm, held_hbm, gi_hbm, gids, bs_hbm, bh_hbm,
    out_hbm, gout_hbm,
    xin, w, sent, held, gi, bs, bh, xg, pbuf, m1, m2, wout, win, obuf, gwout, gwin, gobuf,
    table, oha, ohg, st_out, st_in, mean_l, rstd_l,
    lsem, osem, gosem, ag_s, ag_r, m1_s, m1_r, m2_s, m2_r, wr_s, wr_r, gw_s, gw_r, st_s, st_r,
):
    s = lax.axis_index("section")
    d = lax.axis_index("dp")
    t = lax.axis_index("tensor")
    y = t // 4
    zl = (t // 2) % 2
    c = t % 2
    yn, yp = (y + 1) % 4, (y + 3) % 4
    y2 = (y + 2) % 4

    def dev(ds=0, dd=0, y_=None, zl_=None, c_=None):
        y_ = y if y_ is None else y_
        zl_ = zl if zl_ is None else zl_
        c_ = c if c_ is None else c_
        return ((s + ds) % 4, (d + dd) % 4, y_ * 4 + zl_ * 2 + c_)

    z_peer = dev(zl_=1 - zl)
    y_next, y_prev = dev(y_=yn), dev(y_=yp)
    sibling = dev(c_=1 - c)

    loads = [
        pltpu.make_async_copy(a, b, lsem.at[i])
        for i, (a, b) in enumerate(
            (
                (x_hbm, xin), (gi_hbm, gi), (bs_hbm, bs), (w_hbm, w),
                (sent_hbm, sent), (held_hbm, held), (bh_hbm, bh),
            )
        )
    ]
    for load in loads:
        load.start()

    barrier = pltpu.get_barrier_semaphore()
    peers = [z_peer, y_next, y_prev, sibling, dev(dd=1), dev(dd=2), dev(dd=3), dev(ds=1), dev(ds=3)]
    for peer in peers:
        pl.semaphore_signal(barrier, inc=1, device_id=peer, device_id_type=MESH)

    row = lax.broadcasted_iota(jnp.int32, (HB, HB), 0)
    lane = lax.broadcasted_iota(jnp.int32, (HB, HB), 1)
    both = row & lane
    both = both ^ (both >> 4)
    both = both ^ (both >> 2)
    both = both ^ (both >> 1)
    signs = (1 - 2 * (both & 1)).astype(f32)
    table[0:HB] = signs.astype(bf16)
    table[HB : 2 * HB] = signs.astype(bf16)
    table[2 * HB : 3 * HB] = (-signs).astype(bf16)
    lane_f = lane.astype(f32)

    def picked(ids_row):
        column = jnp.transpose(jnp.broadcast_to(ids_row.astype(f32), (HB, HB)))
        return jnp.where(column == lane_f, 1.0, 0.0).astype(bf16)

    for q in range(4):
        oha[q] = picked(aids[q : q + 1, :])
    ohg[...] = picked(gids[0:1, :])

    loads[0].wait()

    def stat(i, carry):
        rows = pl.ds(pl.multiple_of(i * 16, 16), 16)
        v = xin[rows, :].astype(f32)
        mean_l[rows, :] = jnp.broadcast_to(jnp.sum(v, axis=1, keepdims=True), (16, HB))
        rstd_l[rows, :] = jnp.broadcast_to(jnp.sum(v * v, axis=1, keepdims=True), (16, HB))
        return carry

    lax.fori_loop(0, TR // 16, stat, 0)
    packed = jnp.where(lane == 0, mean_l[...], rstd_l[...])
    st_out[...] = jnp.transpose(packed)[0:8, :]
    pl.semaphore_wait(barrier, len(peers))

    def st_copy(j):
        return pltpu.make_async_remote_copy(
            src_ref=st_out, dst_ref=st_in.at[j], send_sem=st_s.at[j], recv_sem=st_r.at[j],
            device_id=dev(dd=j + 1), device_id_type=MESH,
        )

    for j in range(3):
        st_copy(j).start()
    for j in range(3):
        st_copy(j).wait_recv()
    total = st_out[...] + st_in[0] + st_in[1] + st_in[2]
    mean = total[0:1, :] * (1.0 / D)
    var = total[1:2, :] * (1.0 / D) - mean * mean
    rstd = lax.rsqrt(var + epsilon)
    mean_l[...] = jnp.transpose(jnp.broadcast_to(mean, (HB, HB)))
    rstd_l[...] = jnp.transpose(jnp.broadcast_to(rstd, (HB, HB)))

    def slot(c_, y_, zl_):
        return pl.ds(pl.multiple_of(c_ * PLANE + y_ * (2 * PR) + zl_ * PR, PR), PR)

    def group(c_, y_):
        return pl.ds(pl.multiple_of(c_ * PLANE + y_ * (2 * PR), 2 * PR), 2 * PR)

    sends = (
        (slot(c, y, zl), z_peer),
        (slot(c, y, zl), y_next),
        (slot(c, y, zl), y_prev),
        (slot(c, y, 1 - zl), y_next),
        (slot(c, y, 1 - zl), y_prev),
        (slot(c, yp, 1), y_next),
        (slot(c, yn, 0), y_prev),
        (group(c, y), sibling),
        (group(c, yp), sibling),
        (group(c, yn), sibling),
        (group(c, y2), sibling),
    )
    comes = (
        slot(c, y, 1 - zl),
        slot(c, yp, zl),
        slot(c, yn, zl),
        slot(c, yp, 1 - zl),
        slot(c, yn, 1 - zl),
        slot(c, y2, 1),
        slot(c, y2, 0),
        group(1 - c, y),
        group(1 - c, yp),
        group(1 - c, yn),
        group(1 - c, y2),
    )

    def ag(kind, p):
        rows, peer = sends[kind]
        return pltpu.make_async_remote_copy(
            src_ref=xg.at[p, rows], dst_ref=xg.at[p, rows],
            send_sem=ag_s.at[p, kind], recv_sem=ag_r.at[p, kind],
            device_id=peer, device_id_type=MESH,
        )

    def ag_wait(kind, p):
        rows, peer = comes[kind], sends[kind][1]
        pltpu.make_async_remote_copy(
            src_ref=xg.at[p, rows], dst_ref=xg.at[p, rows],
            send_sem=ag_s.at[p, kind], recv_sem=ag_r.at[p, kind],
            device_id=peer, device_id_type=MESH,
        ).wait_recv()

    def half(h, dest):
        return pl.ds(pl.multiple_of(h * PLANE + dest * (2 * PR), 2 * PR), 2 * PR)

    dn, dq, d2 = (d + 1) % 4, (d + 3) % 4, (d + 2) % 4

    def first(way, p):
        return pltpu.make_async_remote_copy(
            src_ref=pbuf.at[p, half(1 - way, d2)], dst_ref=m1.at[p, way],
            send_sem=m1_s.at[p, way], recv_sem=m1_r.at[p, way],
            device_id=dev(dd=1 if way == 0 else 3), device_id_type=MESH,
        )

    def second(way, h, p):
        return pltpu.make_async_remote_copy(
            src_ref=pbuf.at[p, half(h, dn if way == 0 else dq)], dst_ref=m2.at[p, way, h],
            send_sem=m2_s.at[p, way, h], recv_sem=m2_r.at[p, way, h],
            device_id=dev(dd=1 if way == 0 else 3), device_id_type=MESH,
        )

    def wire(p):
        return pltpu.make_async_remote_copy(
            src_ref=wout.at[p], dst_ref=win.at[p], send_sem=wr_s.at[p], recv_sem=wr_r.at[p],
            device_id=dev(ds=1), device_id_type=MESH,
        )

    def grad_wire(g):
        return pltpu.make_async_remote_copy(
            src_ref=gwout.at[g], dst_ref=gwin.at[g], send_sem=gw_s.at[g], recv_sem=gw_r.at[g],
            device_id=dev(ds=3), device_id_type=MESH,
        )

    def out_copy(p):
        rows = pl.ds(pl.multiple_of(p * PR, PR), PR)
        return pltpu.make_async_copy(obuf.at[:, rows], out_hbm.at[:, rows], osem.at[p])

    def gout_copy(g):
        columns = pl.ds(pl.multiple_of(g * GC, GC), GC)
        return pltpu.make_async_copy(gobuf.at[:, columns], gout_hbm.at[:, columns], gosem.at[g])

    def own_rows(p):
        rows = pl.ds(pl.multiple_of(p * PR, PR), PR)
        return jnp.concatenate([oha[0, rows], oha[2, rows], oha[1, rows], oha[3, rows]], axis=0)

    def stage_own(p):
        rows = pl.ds(pl.multiple_of(p * PR, PR), PR)
        v = xin[rows, :].astype(f32)
        v = (v - mean_l[rows, 0:1]) * rstd_l[rows, 0:1] * gain[...] + shift[...]
        xg[p, slot(c, y, zl), :] = v.astype(bf16)
        for kind in (0, 1, 2):
            ag(kind, p).start()

    def stage_near(p):
        ag_wait(0, p)
        ag(3, p).start()
        ag(4, p).start()
        ag(7, p).start()
        ag_wait(1, p)
        ag_wait(2, p)

        @pl.when(zl == 1)
        def _():
            ag(5, p).start()

        @pl.when(zl == 0)
        def _():
            ag(6, p).start()

    def stage_far(p):
        ag_wait(3, p)
        ag_wait(4, p)

        @pl.when(zl == 0)
        def _():
            ag(5, p).start()

        @pl.when(zl == 1)
        def _():
            ag(6, p).start()

        ag(8, p).start()
        ag(9, p).start()

    def stage_opposite(p):
        ag_wait(5, p)
        ag_wait(6, p)
        ag(10, p).start()

    def stage_product(p):
        for kind in (7, 8, 9, 10):
            ag_wait(kind, p)
        pbuf[p] = dot(xg[p], w[...]).astype(bf16)
        first(0, p).start()
        first(1, p).start()
        second(0, 0, p).start()
        second(1, 1, p).start()

    def stage_sum(p):
        for way in (0, 1):
            first(way, p).wait_recv()
            rows = half(1 - way, dn if way == 0 else dq)
            pbuf[p, rows, :] = (pbuf[p, rows, :].astype(f32) + m1[p, way].astype(f32)).astype(bf16)
            second(way, 1 - way, p).start()

    def stage_code(p):
        for way in (0, 1):
            for h in (0, 1):
                second(way, h, p).wait_recv()
        parts = []
        for h in (0, 1):
            parts.append(
                pbuf[p, half(h, d), :].astype(f32) + m2[p, 0, h].astype(f32) + m2[p, 1, h].astype(f32)
            )
        delta = jnp.concatenate(parts, axis=0) + bias[...] - dot(own_rows(p), sent[...])
        for b in range(ND // HB):
            columns = slice(b * HB, (b + 1) * HB)
            high = delta[:, columns].astype(bf16)
            low = (delta[:, columns] - high.astype(f32)).astype(bf16)
            tu = dot(jnp.concatenate([high, low], axis=1), table[0 : 2 * HB])
            wout[p, :, columns] = clipped(tu)
        wire(p).start()

    def stage_decode(p):
        wire(p).wait_recv()
        chosen = own_rows(p)
        rows = pl.ds(pl.multiple_of(p * PR, PR), PR)
        for b in range(ND // HB):
            columns = slice(b * HB, (b + 1) * HB)
            value = dot(
                jnp.concatenate([chosen, win[p, :, columns]], axis=1),
                jnp.concatenate([held[:, columns], table[0:HB]], axis=0),
            ).astype(bf16)
            for i, q in enumerate((0, 2, 1, 3)):
                obuf[q, rows, columns] = value[i * PR : (i + 1) * PR]
        out_copy(p).start()

    def stage_grad(g):
        for b in range(GB):
            columns = pl.ds(pl.multiple_of(g * GC + b * HB, HB), HB)
            stored = dot(ohg[...], bs[:, columns]).astype(bf16)
            tu = dot(jnp.concatenate([gi[:, columns], stored], axis=1), table[HB : 3 * HB])
            gwout[g, :, b * HB : (b + 1) * HB] = clipped(tu)
        grad_wire(g).start()

    def stage_grad_decode(g):
        grad_wire(g).wait_recv()
        for b in range(GB):
            columns = pl.ds(pl.multiple_of(g * GC + b * HB, HB), HB)
            gobuf[:, columns] = dot(
                jnp.concatenate([ohg[...], gwin[g, :, b * HB : (b + 1) * HB]], axis=1),
                jnp.concatenate([bh[:, columns], table[0:HB]], axis=0),
            ).astype(bf16)
        gout_copy(g).start()

    def at(k, delay, stage, count=PIECES):
        p = k - delay

        @pl.when((p >= 0) & (p < count))
        def _():
            stage(p)

    def tick(k, carry):
        at(k, 0, stage_own)
        at(k, 1, stage_near)
        at(k, 2, stage_far)
        at(k, 3, stage_opposite)

        @pl.when(k == 0)
        def _():
            loads[1].wait()
            loads[2].wait()

        @pl.when(k == 4)
        def _():
            for i in (3, 4, 5, 6):
                loads[i].wait()

        at(k, 4, stage_product)
        at(k, 5, stage_sum)
        at(k, 6, stage_code)
        at(k, 7, stage_decode)
        at(k, 0, stage_grad, GSTEPS)
        at(k, 5, stage_grad_decode, GSTEPS)
        return carry

    lax.fori_loop(0, PIECES + 7, tick, 0)

    for j in range(3):
        st_copy(j).wait_send()

    def finish(p, carry):
        for kind in range(11):
            ag(kind, p).wait_send()
        for way in (0, 1):
            first(way, p).wait_send()
            for h in (0, 1):
                second(way, h, p).wait_send()
        wire(p).wait_send()
        out_copy(p).wait()
        return carry

    lax.fori_loop(0, PIECES, finish, 0)

    def finish_grad(g, carry):
        grad_wire(g).wait_send()
        gout_copy(g).wait()
        return carry

    lax.fori_loop(0, GSTEPS, finish_grad, 0)


def shards(
    act_input, ln_gain, ln_shift, w_proj, b_proj, act_ids, sent_copy, held_copy,
    grad_input, grad_ids, back_sent, back_held,
):
    anywhere = pl.BlockSpec(memory_space=pl.ANY)
    vmem = pl.BlockSpec(memory_space=pltpu.VMEM)
    dma = pltpu.SemaphoreType.DMA
    arrived, grad_arrived = pl.pallas_call(
        kernel,
        out_shape=(
            jax.ShapeDtypeStruct((4, TR, ND), bf16),
            jax.ShapeDtypeStruct((TR, KD), bf16),
        ),
        in_specs=[
            anywhere, vmem, vmem, anywhere, vmem, vmem, anywhere, anywhere, anywhere, vmem, anywhere, anywhere,
        ],
        out_specs=(anywhere, anywhere),
        scratch_shapes=[
            pltpu.VMEM((TR, KD), bf16),
            pltpu.VMEM((KD, ND), bf16),
            pltpu.VMEM((HB, ND), bf16),
            pltpu.VMEM((HB, ND), bf16),
            pltpu.VMEM((TR, KD), bf16),
            pltpu.VMEM((HB, KD), bf16),
            pltpu.VMEM((HB, KD), bf16),
            pltpu.VMEM((PIECES, 2 * PLANE, KD), bf16),
            pltpu.VMEM((PIECES, 2 * PLANE, ND), bf16),
            pltpu.VMEM((PIECES, 2, 2 * PR, ND), bf16),
            pltpu.VMEM((PIECES, 2, 2, 2 * PR, ND), bf16),
            pltpu.VMEM((PIECES, 4 * PR, ND), bf16),
            pltpu.VMEM((PIECES, 4 * PR, ND), bf16),
            pltpu.VMEM((4, TR, ND), bf16),
            pltpu.VMEM((GSTEPS, TR, GC), bf16),
            pltpu.VMEM((GSTEPS, TR, GC), bf16),
            pltpu.VMEM((TR, KD), bf16),
            pltpu.VMEM((3 * HB, HB), bf16),
            pltpu.VMEM((4, TR, HB), bf16),
            pltpu.VMEM((TR, HB), bf16),
            pltpu.VMEM((8, HB), f32),
            pltpu.VMEM((3, 8, HB), f32),
            pltpu.VMEM((TR, HB), f32),
            pltpu.VMEM((TR, HB), f32),
            dma((7,)),
            dma((PIECES,)),
            dma((GSTEPS,)),
            dma((PIECES, 11)),
            dma((PIECES, 11)),
            dma((PIECES, 2)),
            dma((PIECES, 2)),
            dma((PIECES, 2, 2)),
            dma((PIECES, 2, 2)),
            dma((PIECES,)),
            dma((PIECES,)),
            dma((GSTEPS,)),
            dma((GSTEPS,)),
            dma((3,)),
            dma((3,)),
        ],
        compiler_params=pltpu.CompilerParams(
            collective_id=0, has_side_effects=True, vmem_limit_bytes=56 * 2**20
        ),
        cost_estimate=pl.CostEstimate(
            flops=2 * 2048 * KD * ND, bytes_accessed=14 * 2**20, transcendentals=0
        ),
        name="relay",
    )(
        act_input[0], ln_gain, ln_shift, w_proj[0], b_proj, act_ids.reshape(4, TR),
        sent_copy[0], held_copy[0], grad_input[0], grad_ids.reshape(1, TR), back_sent[0], back_held[0],
    )
    return (arrived.reshape(1, 4 * TR, ND), grad_arrived[None])


def solution(mesh):
    placed = (
        P("section", "tensor", "dp"),
        P("section", "dp"),
        P("section", "dp"),
        P("section", "dp", "tensor"),
        P("section", "tensor"),
        P("dp"),
        P("section", "dp", "tensor"),
        P("section", "dp", "tensor"),
        P("section", "tensor", "dp"),
        P("tensor"),
        P("section", "tensor", "dp"),
        P("section", "tensor", "dp"),
    )
    return jax.shard_map(
        shards,
        mesh=mesh,
        in_specs=placed,
        out_specs=(P("section", "dp", "tensor"), P("section", "tensor", "dp")),
        check_vma=False,
    )
```

time: 253 us -> 125 us (0.49)
  waiting for transfers between devices: 155 us -> 0 us
  Pallas kernels: 0 us -> 120 us
  matrix products: 32.6 us -> 0 us
  blocking collectives: 14 us -> 0 us
  between operations: 14.3 us -> 0.64 us
  local copies, waits for them, and re-layouts: 16.4 us -> 4.33 us
  other arithmetic: 12 us -> 0 us
  starting transfers between devices: 6.71 us -> 0 us
    pallas_call x0 -> x1, Pallas kernels: none -> 120 us  [shards(): pl.pallas_call(kernel, out_shape=(jax.ShapeDtypeStruct((4, TR, ND), bf16)...]
    all_gather x1 -> x0, waiting for transfers between devices: 83.1 us -> none  [shards(): lax.all_gather(normed, 'tensor', axis=0, tiled=True)]
    reduce_scatter x1 -> x0, waiting for transfers between devices: 40.8 us -> none  [shards(): lax.psum_scatter(partial_value.astype(jnp.bfloat16), 'dp', scatter_dimens...]
    dot_general x5 -> x0, matrix products: 32.6 us -> none  [the longest x1 20.7 us: shards(): jnp.dot(lax.all_gather(normed, 'tensor', axis=0, tiled=True), weights, pr...]
    ppermute x4 -> x0, waiting for transfers between devices: 31.1 us -> none  [from_behind(): return lax.ppermute(value, axis, pairs)]
    psum x1 -> x0, blocking collectives: 14 us -> none  [shards(): lax.psum((jnp.sum(values, axis=1), jnp.sum(values * values, axis=1)), 'dp')]
    gather x4 -> x0, local copies, waits for them, and re-layouts: 8.61 us -> none  [the longest x1 2.74 us: shards(): delta = output - jnp.take(sent_copy[0], act_ids, axis=0).astype(jnp.float32)]
    ppermute x4 -> x0, starting transfers between devices: 6.63 us -> none  [from_behind(): return lax.ppermute(value, axis, pairs)]
  transfers between devices with their start and end apart: 6 -> 0, of which waited for: 4 -> 0; matrix products, arithmetic and copies ran while one was open for 8% -> 0% of each run, Pallas kernels for 0% -> 0%
where the time goes in v1:
time: 125 us
  Pallas kernels  120 us (96%)
  local copies, waits for them, and re-layouts  4.33 us (3%)
    pallas_call x1, Pallas kernels, shards(): pl.pallas_call(kernel, out_shape=(jax.ShapeDtypeStruct((4, TR, ND), bf16)...  120 us
    unnamed x2, local copies, waits for them, and re-layouts  4.33 us

profile of v1, /device:TPU:32, one launch (start us, length us, event | category | flops | bytes accessed | tf_op | source)
XLA Modules:
  0.0 125.0 jit_solution(8433431973671162973)
XLA Ops:
  0.6 120.1 %relay.1 = (bf16[4,128,896]{2,1,0:T(8,128)(2,1)}, bf16[128,3584]{1,0:T(8,128)(2,1)}) custom-call(bf16[128,3584]{1,0:T(8,128)(2,1)} %bitcast.14, f32[1,3584]{1,0:T(1,128)} %gain.1, f32[1,3584]{1,0:T(1,128)} %shift.1, bf16[3584,896]{1,0:T(8,128)(2,1)} %bitcast.13, f32[1,896]{1,0:T(1,128)} %bias.1, s32[4,128]{1,0:T(4,128)} %bitcast.20, ...), custom_call_target="tpu_custom_call" | custom-call | flops 13153337344 | bytes 14680064 | tf_op jit(solution)/shard_map/relay/pallas_call | solution.py:403
  120.7 2.2 %copy.16 = bf16[1,512,896]{2,1,0:T(8,128)(2,1)} copy(bf16[1,512,896]{2,1,0:T(8,128)(2,1)} %bitcast.12) | data formatting | bytes 1835008
  122.9 2.2 %copy.17 = bf16[1,128,3584]{2,1,0:T(8,128)(2,1)} copy(bf16[1,128,3584]{2,1,0:T(8,128)(2,1)} %bitcast.11) | data formatting | bytes 1835008

commit v2 on v1

v2 whole, which is shorter than its diff:
```python
import functools
import math

import jax
import jax.numpy as jnp
from jax import lax
from jax.experimental import pallas as pl
from jax.experimental.pallas import tpu as pltpu
from jax.sharding import PartitionSpec as P

D = 14336
HB = 128
KD = 3584
ND = 896
TR = 128
PIECES = 8
PR = TR // PIECES
PLANE = 8 * PR
GB = 4
GSTEPS = KD // (HB * GB)
GC = GB * HB
AHEAD = 2
CODE_DELAY = 4
GRAD_DELAY = 1
PARTS = ((0, 512), (512, 384))

epsilon = 1e-05
scale_epsilon = 1e-06
clip_level = 2.5

MESH = pl.DeviceIdType.MESH
f32 = jnp.float32
bf16 = jnp.bfloat16


def dot(a, b):
    return jnp.dot(a, b, preferred_element_type=f32)


def clipped(tu):
    mean = jnp.sum(tu * tu, axis=1, keepdims=True) * (1.0 / (HB * HB))
    scale = jnp.sqrt(mean + scale_epsilon).astype(bf16).astype(f32)
    bound = scale * (clip_level / math.sqrt(HB))
    return jnp.clip(tu * (1.0 / HB), -bound, bound).astype(bf16)


def kernel(
    x_hbm, gain_hbm, shift_hbm, w_hbm, bias_hbm, aids_hbm, sent_hbm, held_hbm, gi_hbm, gids_hbm, bs_hbm, bh_hbm,
    obuf, gobuf,
    xin, gain, shift, bias, aids, gids, w, sent, held, gi, bs, bh, xr, xg, pbuf, m1, m2, wout, win, gwout, gwin,
    table, oha, ohg, st_out, st_in, tok_out, tok_in, stat_t,
    lsem, ag_s, ag_r, m1_s, m1_r, m2_s, m2_r, wr_s, wr_r, gw_s, gw_r, st_s, st_r, tok_s, tok_r,
):
    s = lax.axis_index("section")
    d = lax.axis_index("dp")
    t = lax.axis_index("tensor")
    y = t // 4
    zl = (t // 2) % 2
    c = t % 2
    yn, yp = (y + 1) % 4, (y + 3) % 4
    y2 = (y + 2) % 4

    def dev(ds=0, dd=0, y_=None, zl_=None, c_=None):
        y_ = y if y_ is None else y_
        zl_ = zl if zl_ is None else zl_
        c_ = c if c_ is None else c_
        return ((s + ds) % 4, (d + dd) % 4, y_ * 4 + zl_ * 2 + c_)

    z_peer = dev(zl_=1 - zl)
    y_next, y_prev = dev(y_=yn), dev(y_=yp)
    sibling = dev(c_=1 - c)

    loads = [
        pltpu.make_async_copy(a, b, lsem.at[i])
        for i, (a, b) in enumerate(
            (
                (x_hbm, xin), (aids_hbm, aids), (gids_hbm, gids), (gain_hbm, gain), (shift_hbm, shift), (bias_hbm, bias),
                (gi_hbm, gi), (bs_hbm, bs), (w_hbm, w), (sent_hbm, sent), (held_hbm, held), (bh_hbm, bh),
            )
        )
    ]
    barrier = pltpu.get_barrier_semaphore()
    plane = [(0, 1), (1, 0), (3, 0), (1, 1), (3, 1), (2, 0), (2, 1)]
    plane_peers = [dev(y_=(y + a) % 4, zl_=(zl + b) % 2) for a, b in plane]
    peers = plane_peers + [sibling, dev(dd=1), dev(dd=2), dev(dd=3), dev(ds=1), dev(ds=3)]
    for peer in peers:
        pl.semaphore_signal(barrier, inc=1, device_id=peer, device_id_type=MESH)
    for load in loads[0:6]:
        load.start()

    row = lax.broadcasted_iota(jnp.int32, (HB, HB), 0)
    lane = lax.broadcasted_iota(jnp.int32, (HB, HB), 1)
    both = row & lane
    both = both ^ (both >> 4)
    both = both ^ (both >> 2)
    both = both ^ (both >> 1)
    signs = (1 - 2 * (both & 1)).astype(f32)
    table[0:HB] = signs.astype(bf16)
    table[HB : 2 * HB] = signs.astype(bf16)
    table[2 * HB : 3 * HB] = (-signs).astype(bf16)
    lane_f = lane.astype(f32)

    def picked(ids_row):
        column = jnp.transpose(jnp.broadcast_to(ids_row.astype(f32), (HB, HB)))
        return jnp.where(column == lane_f, 1.0, 0.0).astype(bf16)

    def slot(y_, zl_):
        return pl.ds(pl.multiple_of(y_ * (2 * PR) + zl_ * PR, PR), PR)

    def group(c_, y_):
        return pl.ds(pl.multiple_of(c_ * PLANE + y_ * (2 * PR), 2 * PR), 2 * PR)

    def piece(p):
        return pl.ds(pl.multiple_of(p * PR, PR), PR)

    sends = (
        (None, z_peer),
        (None, y_next),
        (None, y_prev),
        (slot(y, 1 - zl), y_next),
        (slot(y, 1 - zl), y_prev),
        (slot(yp, 1), y_next),
        (slot(yn, 0), y_prev),
        (group(c, y), sibling),
        (group(c, yp), sibling),
        (group(c, yn), sibling),
        (group(c, y2), sibling),
    )
    comes = (
        slot(y, 1 - zl),
        slot(yp, zl),
        slot(yn, zl),
        slot(yp, 1 - zl),
        slot(yn, 1 - zl),
        slot(y2, 1),
        slot(y2, 0),
        group(1 - c, y),
        group(1 - c, yp),
        group(1 - c, yn),
        group(1 - c, y2),
    )

    def ag(kind, p):
        rows, peer = sends[kind]
        buffer = xr if kind < 7 else xg
        if kind < 3:
            rows = slot(y, zl)
            source = x_hbm.at[piece(p)]
        else:
            source = buffer.at[p, rows]
        return pltpu.make_async_remote_copy(
            src_ref=source, dst_ref=buffer.at[p, rows],
            send_sem=ag_s.at[p, kind], recv_sem=ag_r.at[p, kind],
            device_id=peer, device_id_type=MESH,
        )

    def ag_wait(kind, p):
        rows, peer = comes[kind], sends[kind][1]
        buffer = xr if kind < 7 else xg
        pltpu.make_async_remote_copy(
            src_ref=buffer.at[p, rows], dst_ref=buffer.at[p, rows],
            send_sem=ag_s.at[p, kind], recv_sem=ag_r.at[p, kind],
            device_id=peer, device_id_type=MESH,
        ).wait_recv()

    def st_copy(j):
        return pltpu.make_async_remote_copy(
            src_ref=st_out, dst_ref=st_in.at[j], send_sem=st_s.at[j], recv_sem=st_r.at[j],
            device_id=dev(dd=j + 1), device_id_type=MESH,
        )

    def tok_copy(j):
        return pltpu.make_async_remote_copy(
            src_ref=tok_out, dst_ref=tok_in.at[j], send_sem=tok_s.at[j], recv_sem=tok_r.at[j],
            device_id=plane_peers[j], device_id_type=MESH,
        )

    def stat(i, carry):
        rows = pl.ds(pl.multiple_of(i * 16, 16), 16)
        v = xin[rows, :].astype(f32)
        sums = jnp.sum(v, axis=1, keepdims=True)
        squares = jnp.sum(v * v, axis=1, keepdims=True)
        stat_t[0, rows, :] = jnp.where(lane[0:16] == 0, sums, squares)
        return carry

    def stats_send():
        lax.fori_loop(0, TR // 16, stat, 0)
        st_out[...] = jnp.transpose(stat_t[0])[0:8, :]
        for j in range(3):
            st_copy(j).start()

    def stats_total():
        for j in range(3):
            st_copy(j).wait_recv()
        total = st_out[...] + st_in[0] + st_in[1] + st_in[2]
        mean = total[0:1, :] * (1.0 / D)
        var = total[1:2, :] * (1.0 / D) - mean * mean
        rstd = lax.rsqrt(var + epsilon)
        sub = lax.broadcasted_iota(jnp.int32, (8, HB), 0)
        tok_out[...] = jnp.where(sub == 0, mean, rstd)
        for j in range(7):
            tok_copy(j).start()

    def stats_spread(y_, zl_, value):
        rows = jnp.where(row < HB // 2, value[0:1, :], value[1:2, :])
        stat_t[y_ * 2 + zl_] = jnp.transpose(rows)

    def stats_come():
        stats_spread(y, zl, tok_out[...])
        for j, (a, b) in enumerate(plane):
            tok_copy(j).wait_recv()
            stats_spread((y + 4 - a) % 4, (zl + b) % 2, tok_in[j])

    def normalize(y_, zl_, p, values):
        i = y_ * 2 + zl_
        mean, rstd = stat_t[i, piece(p), 0:1], stat_t[i, piece(p), HB // 2 : HB // 2 + 1]
        v = (values.astype(f32) - mean) * rstd * gain[...] + shift[...]
        rows = pl.ds(pl.multiple_of(c * PLANE + y_ * (2 * PR) + zl_ * PR, PR), PR)
        xg[p, rows, :] = v.astype(bf16)

    def half(h, dest):
        return pl.ds(pl.multiple_of(h * PLANE + dest * (2 * PR), 2 * PR), 2 * PR)

    dn, dq, d2 = (d + 1) % 4, (d + 3) % 4, (d + 2) % 4

    def part(f):
        return pl.ds(*PARTS[f])

    def first(way, f, p):
        return pltpu.make_async_remote_copy(
            src_ref=pbuf.at[p, half(1 - way, d2), part(f)], dst_ref=m1.at[p, way, :, part(f)],
            send_sem=m1_s.at[p, way, f], recv_sem=m1_r.at[p, way, f],
            device_id=dev(dd=1 if way == 0 else 3), device_id_type=MESH,
        )

    def second(way, h, f, p):
        return pltpu.make_async_remote_copy(
            src_ref=pbuf.at[p, half(h, dn if way == 0 else dq), part(f)], dst_ref=m2.at[p, way, h, :, part(f)],
            send_sem=m2_s.at[p, way, h, f], recv_sem=m2_r.at[p, way, h, f],
            device_id=dev(dd=1 if way == 0 else 3), device_id_type=MESH,
        )

    def wire(f, p):
        return pltpu.make_async_remote_copy(
            src_ref=wout.at[p, :, part(f)], dst_ref=win.at[p, :, part(f)], send_sem=wr_s.at[p, f], recv_sem=wr_r.at[p, f],
            device_id=dev(ds=1), device_id_type=MESH,
        )

    def grad_wire(g):
        return pltpu.make_async_remote_copy(
            src_ref=gwout.at[g], dst_ref=gwin.at[g], send_sem=gw_s.at[g], recv_sem=gw_r.at[g],
            device_id=dev(ds=3), device_id_type=MESH,
        )

    def own_rows(p):
        rows = pl.ds(pl.multiple_of(p * PR, PR), PR)
        return jnp.concatenate([oha[0, rows], oha[2, rows], oha[1, rows], oha[3, rows]], axis=0)

    def stage_own(p):
        ag(0, p).start()

    def stage_next(p):
        ag(1, p).start()
        ag(2, p).start()

    def stage_near(p):
        ag_wait(0, p)
        ag(3, p).start()
        ag(4, p).start()
        ag_wait(1, p)
        ag_wait(2, p)

        @pl.when(zl == 1)
        def _():
            ag(5, p).start()

        @pl.when(zl == 0)
        def _():
            ag(6, p).start()

    def stage_far(p):
        ag_wait(3, p)
        ag_wait(4, p)

        @pl.when(zl == 0)
        def _():
            ag(5, p).start()

        @pl.when(zl == 1)
        def _():
            ag(6, p).start()

    def stage_normalize(p):
        normalize(y, zl, p, xin[piece(p), :])
        normalize(y, 1 - zl, p, xr[p, slot(y, 1 - zl), :])
        ag(7, p).start()
        for kind, y_ in ((8, yp), (9, yn)):
            for zl_ in (0, 1):
                normalize(y_, zl_, p, xr[p, slot(y_, zl_), :])
            ag(kind, p).start()

    def stage_opposite(p):
        ag_wait(5, p)
        ag_wait(6, p)
        for zl_ in (0, 1):
            normalize(y2, zl_, p, xr[p, slot(y2, zl_), :])
        ag(10, p).start()

    def stage_product(p):
        for kind in (7, 8, 9, 10):
            ag_wait(kind, p)
        for f in range(2):
            pbuf[p, :, part(f)] = dot(xg[p], w[:, part(f)]).astype(bf16)
            first(0, f, p).start()
            first(1, f, p).start()
            second(0, 0, f, p).start()
            second(1, 1, f, p).start()

    def stage_sum(p):
        for f in range(2):
            for way in (0, 1):
                first(way, f, p).wait_recv()
                rows = half(1 - way, dn if way == 0 else dq)
                pbuf[p, rows, part(f)] = (
                    pbuf[p, rows, part(f)].astype(f32) + m1[p, way, :, part(f)].astype(f32)
                ).astype(bf16)
                second(way, 1 - way, f, p).start()

    def stage_code(p):
        for f in range(2):
            for way in (0, 1):
                for h in (0, 1):
                    second(way, h, f, p).wait_recv()
            parts = []
            for h in (0, 1):
                parts.append(
                    pbuf[p, half(h, d), part(f)].astype(f32)
                    + m2[p, 0, h, :, part(f)].astype(f32)
                    + m2[p, 1, h, :, part(f)].astype(f32)
                )
            delta = jnp.concatenate(parts, axis=0) + bias[:, part(f)] - dot(own_rows(p), sent[:, part(f)])
            for b in range(PARTS[f][1] // HB):
                columns = slice(b * HB, (b + 1) * HB)
                high = delta[:, columns].astype(bf16)
                low = (delta[:, columns] - high.astype(f32)).astype(bf16)
                tu = dot(jnp.concatenate([high, low], axis=1), table[0 : 2 * HB])
                wout[p, :, pl.ds(PARTS[f][0] + b * HB, HB)] = clipped(tu)
            wire(f, p).start()

    def stage_decode(p):
        chosen = own_rows(p)
        rows = pl.ds(pl.multiple_of(p * PR, PR), PR)
        for f in range(2):
            wire(f, p).wait_recv()
            for b in range(PARTS[f][1] // HB):
                columns = pl.ds(PARTS[f][0] + b * HB, HB)
                value = dot(
                    jnp.concatenate([chosen, win[p, :, columns]], axis=1),
                    jnp.concatenate([held[:, columns], table[0:HB]], axis=0),
                ).astype(bf16)
                for i, q in enumerate((0, 2, 1, 3)):
                    obuf[q, rows, columns] = value[i * PR : (i + 1) * PR]

    def stage_grad(g):
        for b in range(GB):
            columns = pl.ds(pl.multiple_of(g * GC + b * HB, HB), HB)
            stored = dot(ohg[...], bs[:, columns]).astype(bf16)
            tu = dot(jnp.concatenate([gi[:, columns], stored], axis=1), table[HB : 3 * HB])
            gwout[g, :, b * HB : (b + 1) * HB] = clipped(tu)
        grad_wire(g).start()

    def stage_grad_decode(g):
        grad_wire(g).wait_recv()
        for b in range(GB):
            columns = pl.ds(pl.multiple_of(g * GC + b * HB, HB), HB)
            gobuf[:, columns] = dot(
                jnp.concatenate([ohg[...], gwin[g, :, b * HB : (b + 1) * HB]], axis=1),
                jnp.concatenate([bh[:, columns], table[0:HB]], axis=0),
            ).astype(bf16)

    def stage_finish(p):
        for kind in range(11):
            ag(kind, p).wait_send()
        for f in range(2):
            for way in (0, 1):
                first(way, f, p).wait_send()
                for h in (0, 1):
                    second(way, h, f, p).wait_send()
            wire(f, p).wait_send()

    def stage_finish_grad(g):
        grad_wire(g).wait_send()

    def at(k, delay, stage, count=PIECES):
        p = k - delay

        @pl.when((p >= 0) & (p < count))
        def _():
            stage(p)

    def tick(k, carry):
        at(k, 2, stage_opposite)
        at(k, 1, stage_far)
        at(k, 0, stage_near)
        at(k, -AHEAD, stage_next)

        @pl.when(k == 0)
        def _():
            stats_total()
            lax.fori_loop(AHEAD, PIECES, own, 0)

        @pl.when(k == 1)
        def _():
            stats_come()

        at(k, 1, stage_normalize)

        @pl.when(k == 2)
        def _():
            for load in loads[8:]:
                load.wait()

        at(k, 2, stage_product)
        at(k, 3, stage_sum)
        at(k, CODE_DELAY, stage_code)
        at(k, CODE_DELAY + 1, stage_decode)
        at(k, GRAD_DELAY, stage_grad, GSTEPS)
        at(k, GRAD_DELAY + 3, stage_grad_decode, GSTEPS)
        at(k, GRAD_DELAY + 4, stage_finish_grad, GSTEPS)
        at(k, CODE_DELAY + 1, stage_finish, PIECES - 1)
        return carry

    def own(p, carry):
        stage_own(p)
        return carry

    pl.semaphore_wait(barrier, len(peers))
    for p in range(AHEAD):
        stage_own(p)
        stage_next(p)
    loads[0].wait()
    stats_send()
    for load in loads[6:]:
        load.start()
    for load in loads[1:6]:
        load.wait()
    for q in range(4):
        oha[q] = picked(aids[q : q + 1, :])
    ohg[...] = picked(gids[0:1, :])
    loads[6].wait()
    loads[7].wait()
    lax.fori_loop(0, PIECES + CODE_DELAY + 1, tick, 0)
    for j in range(7):
        tok_copy(j).wait_send()
    for j in range(3):
        st_copy(j).wait_send()

    stage_finish(PIECES - 1)


def shards(
    act_input, ln_gain, ln_shift, w_proj, b_proj, act_ids, sent_copy, held_copy,
    grad_input, grad_ids, back_sent, back_held,
):
    anywhere = pl.BlockSpec(memory_space=pl.ANY)
    vmem = pl.BlockSpec(memory_space=pltpu.VMEM)
    dma = pltpu.SemaphoreType.DMA
    arrived, grad_arrived = pl.pallas_call(
        kernel,
        out_shape=(
            pltpu.VMEM((4, TR, ND), bf16),
            pltpu.VMEM((TR, KD), bf16),
        ),
        in_specs=[anywhere] * 12,
        out_specs=(vmem, vmem),
        scratch_shapes=[
            pltpu.VMEM((TR, KD), bf16),
            pltpu.VMEM((1, KD), f32),
            pltpu.VMEM((1, KD), f32),
            pltpu.VMEM((1, ND), f32),
            pltpu.VMEM((4, TR), jnp.int32),
            pltpu.VMEM((1, TR), jnp.int32),
            pltpu.VMEM((KD, ND), bf16),
            pltpu.VMEM((HB, ND), bf16),
            pltpu.VMEM((HB, ND), bf16),
            pltpu.VMEM((TR, KD), bf16),
            pltpu.VMEM((HB, KD), bf16),
            pltpu.VMEM((HB, KD), bf16),
            pltpu.VMEM((PIECES, PLANE, KD), bf16),
            pltpu.VMEM((PIECES, 2 * PLANE, KD), bf16),
            pltpu.VMEM((PIECES, 2 * PLANE, ND), bf16),
            pltpu.VMEM((PIECES, 2, 2 * PR, ND), bf16),
            pltpu.VMEM((PIECES, 2, 2, 2 * PR, ND), bf16),
            pltpu.VMEM((PIECES, 4 * PR, ND), bf16),
            pltpu.VMEM((PIECES, 4 * PR, ND), bf16),
            pltpu.VMEM((GSTEPS, TR, GC), bf16),
            pltpu.VMEM((GSTEPS, TR, GC), bf16),
            pltpu.VMEM((3 * HB, HB), bf16),
            pltpu.VMEM((4, TR, HB), bf16),
            pltpu.VMEM((TR, HB), bf16),
            pltpu.VMEM((8, HB), f32),
            pltpu.VMEM((3, 8, HB), f32),
            pltpu.VMEM((8, HB), f32),
            pltpu.VMEM((7, 8, HB), f32),
            pltpu.VMEM((8, TR, HB), f32),
            dma((12,)),
            dma((PIECES, 11)),
            dma((PIECES, 11)),
            dma((PIECES, 2, 2)),
            dma((PIECES, 2, 2)),
            dma((PIECES, 2, 2, 2)),
            dma((PIECES, 2, 2, 2)),
            dma((PIECES, 2)),
            dma((PIECES, 2)),
            dma((GSTEPS,)),
            dma((GSTEPS,)),
            dma((3,)),
            dma((3,)),
            dma((7,)),
            dma((7,)),
        ],
        compiler_params=pltpu.CompilerParams(
            collective_id=0, has_side_effects=True, vmem_limit_bytes=56 * 2**20
        ),
        cost_estimate=pl.CostEstimate(
            flops=2 * 2048 * KD * ND, bytes_accessed=14 * 2**20, transcendentals=0
        ),
        name="relay",
    )(
        act_input[0], ln_gain, ln_shift, w_proj[0], b_proj, act_ids.reshape(4, TR),
        sent_copy[0], held_copy[0], grad_input[0], grad_ids.reshape(1, TR), back_sent[0], back_held[0],
    )
    return (arrived.reshape(1, 4 * TR, ND), grad_arrived[None])


def solution(mesh):
    placed = (
        P("section", "tensor", "dp"),
        P("section", "dp"),
        P("section", "dp"),
        P("section", "dp", "tensor"),
        P("section", "tensor"),
        P("dp"),
        P("section", "dp", "tensor"),
        P("section", "dp", "tensor"),
        P("section", "tensor", "dp"),
        P("tensor"),
        P("section", "tensor", "dp"),
        P("section", "tensor", "dp"),
    )
    return jax.shard_map(
        shards,
        mesh=mesh,
        in_specs=placed,
        out_specs=(P("section", "dp", "tensor"), P("section", "tensor", "dp")),
        check_vma=False,
    )
```

time: 125 us -> 110 us (0.88); the launches traced: 125 us -> 109 us
  Pallas kernels: 120 us -> 106 us
  local copies, waits for them, and re-layouts: 4.33 us -> 1.85 us
    pallas_call x1, Pallas kernels: 120 us -> 106 us  [shards(): pl.pallas_call(kernel, out_shape=(pltpu.VMEM((4, TR, ND), bf16), pltpu.VM...]
    unnamed x2, local copies, waits for them, and re-layouts: 4.33 us -> 1.85 us
where the time goes in v2:
time: 110 us; the launch traced here: 109 us
  Pallas kernels  106 us (96%)
  local copies, waits for them, and re-layouts  1.85 us (2%)
    pallas_call x1, Pallas kernels, shards(): pl.pallas_call(kernel, out_shape=(pltpu.VMEM((4, TR, ND), bf16), pltpu.VM...  106 us

profile of v2, /device:TPU:32, one launch (start us, length us, event | category | flops | bytes accessed | tf_op | source)
XLA Modules:
  0.0 108.7 jit_solution(3627081258271370394)
XLA Ops:
  0.6 106.2 %relay.1 = (bf16[4,128,896]{2,1,0:T(8,128)(2,1)S(1)}, bf16[128,3584]{1,0:T(8,128)(2,1)S(1)}) custom-call(bf16[128,3584]{1,0:T(8,128)(2,1)} %bitcast.14, f32[1,3584]{1,0:T(1,128)} %gain_hbm.1, f32[1,3584]{1,0:T(1,128)} %shift_hbm.1, bf16[3584,896]{1,0:T(8,128)(2,1)} %bitcast.13, f32[1,896]{1,0:T(1,128)} %bias_hbm.1, s32[4,128]{1,0:T(4,128)} %bitcast.20, ...), custom_call_target="tpu_custom_call" | custom-call | flops 13153337344 | bytes 14680064 | tf_op jit(solution)/shard_map/relay/pallas_call | solution.py:468
  106.8 0.9 copy.16
  107.8 0.9 copy.17

commit v3 on v2

--- a/solution.py
+++ b/solution.py
@@ -20,7 +20,7 @@
 GSTEPS = KD // (HB * GB)
 GC = GB * HB
 AHEAD = 2
-CODE_DELAY = 4
+CODE_DELAY = 5
 GRAD_DELAY = 1
 PARTS = ((0, 512), (512, 384))
 
@@ -83,6 +83,7 @@
     plane = [(0, 1), (1, 0), (3, 0), (1, 1), (3, 1), (2, 0), (2, 1)]
     plane_peers = [dev(y_=(y + a) % 4, zl_=(zl + b) % 2) for a, b in plane]
     peers = plane_peers + [sibling, dev(dd=1), dev(dd=2), dev(dd=3), dev(ds=1), dev(ds=3)]
+    peers += [dev(ds=a, dd=b) for a in (1, 3) for b in (1, 3)]
     for peer in peers:
         pl.semaphore_signal(barrier, inc=1, device_id=peer, device_id_type=MESH)
     for load in loads[0:6]:
@@ -237,10 +238,10 @@
         return pltpu.make_async_remote_copy(
             src_ref=pbuf.at[p, half(h, dn if way == 0 else dq), part(f)], dst_ref=m2.at[p, way, h, :, part(f)],
             send_sem=m2_s.at[p, way, h, f], recv_sem=m2_r.at[p, way, h, f],
-            device_id=dev(dd=1 if way == 0 else 3), device_id_type=MESH,
-        )
-
-    def wire(f, p):
+            device_id=dev(ds=1, dd=1 if way == 0 else 3), device_id_type=MESH,
+        )
+
+    def base(f, p):
         return pltpu.make_async_remote_copy(
             src_ref=wout.at[p, :, part(f)], dst_ref=win.at[p, :, part(f)], send_sem=wr_s.at[p, f], recv_sem=wr_r.at[p, f],
             device_id=dev(ds=1), device_id_type=MESH,
@@ -309,12 +310,16 @@
     def stage_product(p):
         for kind in (7, 8, 9, 10):
             ag_wait(kind, p)
+        chosen = own_rows(p)
         for f in range(2):
             pbuf[p, :, part(f)] = dot(xg[p], w[:, part(f)]).astype(bf16)
             first(0, f, p).start()
             first(1, f, p).start()
             second(0, 0, f, p).start()
             second(1, 1, f, p).start()
+            own = jnp.concatenate([pbuf[p, half(0, d), part(f)], pbuf[p, half(1, d), part(f)]], axis=0)
+            wout[p, :, part(f)] = (own.astype(f32) + (bias[:, part(f)] - dot(chosen, sent[:, part(f)]))).astype(bf16)
+            base(f, p).start()
 
     def stage_sum(p):
         for f in range(2):
@@ -327,35 +332,22 @@
                 second(way, 1 - way, f, p).start()
 
     def stage_code(p):
+        chosen = own_rows(p)
+        rows = pl.ds(pl.multiple_of(p * PR, PR), PR)
         for f in range(2):
+            base(f, p).wait_recv()
             for way in (0, 1):
                 for h in (0, 1):
                     second(way, h, f, p).wait_recv()
-            parts = []
-            for h in (0, 1):
-                parts.append(
-                    pbuf[p, half(h, d), part(f)].astype(f32)
-                    + m2[p, 0, h, :, part(f)].astype(f32)
-                    + m2[p, 1, h, :, part(f)].astype(f32)
-                )
-            delta = jnp.concatenate(parts, axis=0) + bias[:, part(f)] - dot(own_rows(p), sent[:, part(f)])
-            for b in range(PARTS[f][1] // HB):
-                columns = slice(b * HB, (b + 1) * HB)
-                high = delta[:, columns].astype(bf16)
-                low = (delta[:, columns] - high.astype(f32)).astype(bf16)
-                tu = dot(jnp.concatenate([high, low], axis=1), table[0 : 2 * HB])
-                wout[p, :, pl.ds(PARTS[f][0] + b * HB, HB)] = clipped(tu)
-            wire(f, p).start()
-
-    def stage_decode(p):
-        chosen = own_rows(p)
-        rows = pl.ds(pl.multiple_of(p * PR, PR), PR)
-        for f in range(2):
-            wire(f, p).wait_recv()
             for b in range(PARTS[f][1] // HB):
                 columns = pl.ds(PARTS[f][0] + b * HB, HB)
+                other = [m2[p, 0, h, :, columns].astype(f32) + m2[p, 1, h, :, columns].astype(f32) for h in (0, 1)]
+                delta = win[p, :, columns].astype(f32) + jnp.concatenate(other, axis=0)
+                high = delta.astype(bf16)
+                low = (delta - high.astype(f32)).astype(bf16)
+                coded = clipped(dot(jnp.concatenate([high, low], axis=1), table[0 : 2 * HB]))
                 value = dot(
-                    jnp.concatenate([chosen, win[p, :, columns]], axis=1),
+                    jnp.concatenate([chosen, coded], axis=1),
                     jnp.concatenate([held[:, columns], table[0:HB]], axis=0),
                 ).astype(bf16)
                 for i, q in enumerate((0, 2, 1, 3)):
@@ -386,7 +378,7 @@
                 first(way, f, p).wait_send()
                 for h in (0, 1):
                     second(way, h, f, p).wait_send()
-            wire(f, p).wait_send()
+            base(f, p).wait_send()
 
     def stage_finish_grad(g):
         grad_wire(g).wait_send()
@@ -423,11 +415,10 @@
         at(k, 2, stage_product)
         at(k, 3, stage_sum)
         at(k, CODE_DELAY, stage_code)
-        at(k, CODE_DELAY + 1, stage_decode)
         at(k, GRAD_DELAY, stage_grad, GSTEPS)
-        at(k, GRAD_DELAY + 3, stage_grad_decode, GSTEPS)
-        at(k, GRAD_DELAY + 4, stage_finish_grad, GSTEPS)
-        at(k, CODE_DELAY + 1, stage_finish, PIECES - 1)
+        at(k, GRAD_DELAY + 2, stage_grad_decode, GSTEPS)
+        at(k, GRAD_DELAY + 3, stage_finish_grad, GSTEPS)
+        at(k, CODE_DELAY, stage_finish, PIECES - 1)
         return carry
 
     def own(p, carry):
@@ -449,7 +440,7 @@
     ohg[...] = picked(gids[0:1, :])
     loads[6].wait()
     loads[7].wait()
-    lax.fori_loop(0, PIECES + CODE_DELAY + 1, tick, 0)
+    lax.fori_loop(0, PIECES + CODE_DELAY, tick, 0)
     for j in range(7):
         tok_copy(j).wait_send()
     for j in range(3):

time: 110 us -> 106 us (0.964)
  Pallas kernels: 106 us -> 102 us
    pallas_call x1, Pallas kernels: 106 us -> 102 us  [shards(): pl.pallas_call(kernel, out_shape=(pltpu.VMEM((4, TR, ND), bf16), pltpu.VM...]
where the time goes in v3:
time: 106 us; the launch traced here: 105 us
  Pallas kernels  102 us (96%)
  local copies, waits for them, and re-layouts  1.85 us (2%)
    pallas_call x1, Pallas kernels, shards(): pl.pallas_call(kernel, out_shape=(pltpu.VMEM((4, TR, ND), bf16), pltpu.VM...  102 us

profile of v3, /device:TPU:32, one launch (start us, length us, event | category | flops | bytes accessed | tf_op | source)
XLA Modules:
  0.0 105.0 jit_solution(2987077586638313756)
XLA Ops:
  0.6 102.5 %relay.1 = (bf16[4,128,896]{2,1,0:T(8,128)(2,1)S(1)}, bf16[128,3584]{1,0:T(8,128)(2,1)S(1)}) custom-call(bf16[128,3584]{1,0:T(8,128)(2,1)} %bitcast.14, f32[1,3584]{1,0:T(1,128)} %gain_hbm.1, f32[1,3584]{1,0:T(1,128)} %shift_hbm.1, bf16[3584,896]{1,0:T(8,128)(2,1)} %bitcast.13, f32[1,896]{1,0:T(1,128)} %bias_hbm.1, s32[4,128]{1,0:T(4,128)} %bitcast.20, ...), custom_call_target="tpu_custom_call" | custom-call | flops 13153337344 | bytes 14680064 | tf_op jit(solution)/shard_map/relay/pallas_call | solution.py:459
  103.1 0.9 copy.16
  104.0 0.9 copy.17

commit v4 on v3

--- a/solution.py
+++ b/solution.py
@@ -315,8 +315,10 @@
             pbuf[p, :, part(f)] = dot(xg[p], w[:, part(f)]).astype(bf16)
             first(0, f, p).start()
             first(1, f, p).start()
+        for f in range(2):
             second(0, 0, f, p).start()
             second(1, 1, f, p).start()
+        for f in range(2):
             own = jnp.concatenate([pbuf[p, half(0, d), part(f)], pbuf[p, half(1, d), part(f)]], axis=0)
             wout[p, :, part(f)] = (own.astype(f32) + (bias[:, part(f)] - dot(chosen, sent[:, part(f)]))).astype(bf16)
             base(f, p).start()
@@ -413,11 +415,11 @@
                 load.wait()
 
         at(k, 2, stage_product)
-        at(k, 3, stage_sum)
-        at(k, CODE_DELAY, stage_code)
         at(k, GRAD_DELAY, stage_grad, GSTEPS)
         at(k, GRAD_DELAY + 2, stage_grad_decode, GSTEPS)
         at(k, GRAD_DELAY + 3, stage_finish_grad, GSTEPS)
+        at(k, 3, stage_sum)
+        at(k, CODE_DELAY, stage_code)
         at(k, CODE_DELAY, stage_finish, PIECES - 1)
         return carry
 

time: 106 us -> 105 us (level)
  no operation moved by 1% of the time
where the time goes in v4:
time: 105 us
  Pallas kernels  102 us (97%)
  local copies, waits for them, and re-layouts  1.85 us (2%)
    pallas_call x1, Pallas kernels, shards(): pl.pallas_call(kernel, out_shape=(pltpu.VMEM((4, TR, ND), bf16), pltpu.VM...  102 us

profile of v4, /device:TPU:32, one launch (start us, length us, event | category | flops | bytes accessed | tf_op | source)
XLA Modules:
  0.0 104.9 jit_solution(11388566398965521825)
XLA Ops:
  0.6 102.4 %relay.1 = (bf16[4,128,896]{2,1,0:T(8,128)(2,1)S(1)}, bf16[128,3584]{1,0:T(8,128)(2,1)S(1)}) custom-call(bf16[128,3584]{1,0:T(8,128)(2,1)} %bitcast.14, f32[1,3584]{1,0:T(1,128)} %gain_hbm.1, f32[1,3584]{1,0:T(1,128)} %shift_hbm.1, bf16[3584,896]{1,0:T(8,128)(2,1)} %bitcast.13, f32[1,896]{1,0:T(1,128)} %bias_hbm.1, s32[4,128]{1,0:T(4,128)} %bitcast.20, ...), custom_call_target="tpu_custom_call" | custom-call | flops 13153337344 | bytes 14680064 | tf_op jit(solution)/shard_map/relay/pallas_call | solution.py:461
  103.1 0.9 copy.16
  104.0 0.9 copy.17
